TPU v7x, 32 devices: a whole 2x2x4 slice. The times are simulated.
32 devices in a mesh: dp: 4 (over y, x), section: 2 (over core), tensor: 4 (over z).
Axes of the slice: x: 2, y: 2, z: 4, core: 2. Of those that a mesh axis runs over, the one named last changes fastest.
Arguments:
- fwd_state: bfloat16 [2, 512, 4096], P('section', ('dp', 'tensor')), may hold values from -6 to 6
- bwd_state: bfloat16 [2, 512, 4096], P('section', ('dp', 'tensor')), may hold values from -6 to 6
- stash: bfloat16 [2, 2, 512, 4096], P('section', None, ('dp', 'tensor')), may hold values from -6 to 6
- gains: bfloat16 [2, 2, 4096], P('section'), may hold values from 0.25 to 1.75
- w_query: bfloat16 [2, 2, 4096, 4096], P('section', None, 'dp', 'tensor'), may hold values from -0.09375 to 0.09375
- w_key: bfloat16 [2, 2, 4096, 1024], P('section', None, 'dp', 'tensor'), may hold values from -0.09375 to 0.09375
- w_value: bfloat16 [2, 2, 4096, 1024], P('section', None, 'dp', 'tensor'), may hold values from -0.09375 to 0.09375
- w_out: bfloat16 [2, 2, 4096, 4096], P('section', None, 'tensor', 'dp'), may hold values from -0.09375 to 0.09375
- fwd_segments: int32 [2, 4, 128], P(None, 'dp'), may hold values from 0 to 3, never falling along the last dimension, each value on 1 to 64 neighbouring positions
- bwd_segments: int32 [2, 4, 128], P(None, 'dp'), may hold values from 0 to 3, never falling along the last dimension, each value on 1 to 64 neighbouring positions
Outputs:
- fwd_out: bfloat16 [2, 512, 4096], P('section', ('dp', 'tensor'))
- bwd_out: bfloat16 [2, 512, 4096], P('section', ('dp', 'tensor'))
- gain_grad: float32 [2, 2, 4096], P('section')
Inputs may be any that keep to these rules, and one draw needn't show every extreme that they name: `fwd_segments`: in each replica's rows of each micro-batch the document ids never fall; each document has at most 64 rows and one has exactly that many. `bwd_segments`: in each replica's rows of each micro-batch the document ids never fall; each document has at most 64 rows and one has exactly that many.
All inputs are finite; a program needn't handle non-finite values.
Results may differ from a plain program's by a relative error of at most 0.02.
Values may be sent and summed in bfloat16 or wider, within the bound.
A program may use at most 192 MiB of HBM per device.

v0:
```python
import math

import jax
import jax.numpy as jnp
from jax import lax
from jax.sharding import PartitionSpec as P

HD = 128
TICKS = 2


ROPE_BASE = 1000000.0


def from_behind(value, axis, steps):
    count = lax.axis_size(axis)
    pairs = [(source, (source + steps) % count) for source in range(count)]
    return lax.ppermute(value, axis, pairs)


def rope_tables(segments):
    count_rows = segments.shape[0]
    row_index = jnp.arange(count_rows, dtype=jnp.int32)
    previous = jnp.concatenate([segments[:1] - 1, segments[:-1]])
    doc_starts = lax.cummax(jnp.where(segments != previous, row_index, 0), axis=0)
    positions = (row_index - doc_starts).astype(jnp.float32)
    halfway = HD // 2
    frequency = jnp.exp(jnp.arange(halfway, dtype=jnp.float32) * (-2.0 * math.log(ROPE_BASE) / HD))
    angles = positions[:, None] * frequency[None, :]
    cosine = jnp.concatenate([jnp.cos(angles), jnp.cos(angles)], axis=1)
    sine_table = jnp.concatenate([jnp.sin(angles), jnp.sin(angles)], axis=1)
    allowed = (segments[:, None] == segments[None, :]) & (row_index[:, None] >= row_index[None, :])
    return (cosine[:, None, :], sine_table[:, None, :], allowed)


def rotate(vectors, cosine, sine_table):
    halfway = vectors.shape[-1] // 2
    turned = jnp.concatenate([-vectors[..., halfway:], vectors[..., :halfway]], axis=-1)
    return vectors * cosine + turned * sine_table


def partial_layer(state_rows, gain_vector, w_query, w_key, w_value, w_out, segments):
    count_rows = state_rows.shape[0]
    cosine, sine_table, allowed = rope_tables(segments)
    variance = jnp.mean(state_rows * state_rows, axis=1, keepdims=True)
    normed = (state_rows * lax.rsqrt(variance + 1e-06) * gain_vector).astype(jnp.bfloat16)
    query_rows = jnp.dot(normed, w_query, preferred_element_type=jnp.float32).reshape(
        count_rows, -1, HD
    )
    key_rows = jnp.dot(normed, w_key, preferred_element_type=jnp.float32).reshape(
        count_rows, -1, HD
    )
    value_rows = jnp.dot(normed, w_value, preferred_element_type=jnp.float32).astype(jnp.bfloat16)
    value_rows = value_rows.reshape(count_rows, -1, HD)
    query_rows = rotate(query_rows, cosine, sine_table).astype(jnp.bfloat16)
    key_rows = rotate(key_rows, cosine, sine_table).astype(jnp.bfloat16)
    key_heads = key_rows.shape[1]
    grouped = query_rows.reshape(count_rows, key_heads, -1, HD)
    scores = jnp.einsum("qkgd,skd->kgqs", grouped.astype(jnp.float32), key_rows.astype(jnp.float32))
    scores = scores * (1.0 / math.sqrt(HD))
    scores = jnp.where(allowed[None, None], scores, -1e30)
    exponents = jnp.exp(scores)
    soft_weights = (exponents / jnp.sum(exponents, axis=-1, keepdims=True)).astype(jnp.bfloat16)
    mixed_heads = jnp.einsum(
        "kgqs,skd->qkgd", soft_weights.astype(jnp.float32), value_rows.astype(jnp.float32)
    )
    mixed_heads = mixed_heads.astype(jnp.bfloat16).reshape(count_rows, -1)
    return jnp.dot(mixed_heads, w_out, preferred_element_type=jnp.float32)


def pick_span(table, span):
    return lax.dynamic_index_in_dim(table, span, 0, keepdims=False)


def per_device(
    fwd_state, bwd_state, stash, gains, w_query, w_key, w_value, w_out, fwd_segments, bwd_segments
):
    phase_count = lax.axis_size("section")
    phase_index = lax.axis_index("section")
    model_width = fwd_state.shape[2]
    query_all, key_all, value_all, out_all = (
        lax.all_gather(w_query, "dp", axis=2, tiled=True),
        lax.all_gather(w_key, "dp", axis=2, tiled=True),
        lax.all_gather(w_value, "dp", axis=2, tiled=True),
        lax.all_gather(w_out, "dp", axis=3, tiled=True),
    )
    stash_full = lax.all_gather(stash, "tensor", axis=2, tiled=True)
    state_rows, grad_rows = (fwd_state[0], bwd_state[0])
    span_ids = jnp.arange(2, dtype=jnp.int32)
    gain_sum = jnp.zeros((2, model_width), jnp.float32)
    for tick_index in range(TICKS):
        full_state, full_grad = (
            lax.all_gather(state_rows, "tensor", axis=0, tiled=True),
            lax.all_gather(grad_rows, "tensor", axis=0, tiled=True),
        )
        fwd_span = jnp.where(phase_index < tick_index, 1, 0).astype(jnp.int32)
        fwd_row = pick_span(fwd_segments[:, 0], (phase_index - tick_index) % phase_count)
        forward_term = partial_layer(
            full_state.astype(jnp.float32),
            pick_span(gains[0], fwd_span).astype(jnp.float32),
            pick_span(query_all[0], fwd_span),
            pick_span(key_all[0], fwd_span),
            pick_span(value_all[0], fwd_span),
            pick_span(out_all[0], fwd_span),
            fwd_row,
        )
        bwd_span = jnp.where(phase_index > phase_count - 1 - tick_index, 0, 1).astype(jnp.int32)
        bwd_row = pick_span(bwd_segments[:, 0], (phase_index + tick_index) % phase_count)
        query_pick = pick_span(query_all[0], bwd_span)
        key_pick = pick_span(key_all[0], bwd_span)
        value_pick = pick_span(value_all[0], bwd_span)
        out_pick = pick_span(out_all[0], bwd_span)

        def local(state_in, gain_in):
            return partial_layer(
                state_in, gain_in, query_pick, key_pick, value_pick, out_pick, bwd_row
            )

        unused, pull = jax.vjp(
            local,
            stash_full[0, tick_index].astype(jnp.float32),
            pick_span(gains[0], bwd_span).astype(jnp.float32),
        )
        backward_term, gain_term = pull(full_grad.astype(jnp.float32))
        chosen = (span_ids == bwd_span).astype(jnp.float32)
        gain_sum = gain_sum + chosen[:, None] * gain_term[None, :]
        forward_sum, backward_sum = (
            lax.psum_scatter(
                forward_term.astype(jnp.bfloat16), "tensor", scatter_dimension=0, tiled=True
            ).astype(jnp.float32),
            lax.psum_scatter(
                backward_term.astype(jnp.bfloat16), "tensor", scatter_dimension=0, tiled=True
            ).astype(jnp.float32),
        )
        advanced = (state_rows.astype(jnp.float32) + forward_sum).astype(jnp.bfloat16)
        returned = (grad_rows.astype(jnp.float32) + backward_sum).astype(jnp.bfloat16)
        state_rows = from_behind(advanced, "section", 1)
        grad_rows = from_behind(returned, "section", -1)
    state_out, grad_out = (state_rows, grad_rows)
    gain_total = lax.psum(gain_sum, ("dp", "tensor"))
    return (state_out[None], grad_out[None], gain_total[None])


def solution(mesh):
    in_specs = (
        P("section", ("dp", "tensor"), None),
        P("section", ("dp", "tensor"), None),
        P("section", None, ("dp", "tensor"), None),
        P("section", None, None),
        P("section", None, "dp", "tensor"),
        P("section", None, "dp", "tensor"),
        P("section", None, "dp", "tensor"),
        P("section", None, "tensor", "dp"),
        P(None, "dp", None),
        P(None, "dp", None),
    )
    out_specs = (
        P("section", ("dp", "tensor"), None),
        P("section", ("dp", "tensor"), None),
        P("section", None, None),
    )
    return jax.shard_map(
        per_device, mesh=mesh, in_specs=in_specs, out_specs=out_specs, check_vma=False
    )
```

profile of v0, /device:TPU:0, one launch (start us, length us, event | category | flops | bytes accessed | tf_op | source)
XLA Modules:
  0.0 853.2 jit_solution(7944280053241273256)
XLA Ops:
  20.4 19.8 %all-gather.26.cloned.1.call-done = bf16[1,128,4096]{2,1,0:T(8,128)(2,1)} async-done(((bf16[1,32,4096]{2,1,0:T(8,128)(2,1)}), bf16[1,128,4096]{2,1,0:T(8,128)(2,1)}) %all-gather.26.cloned.1.call-update) | async-done | bytes 1048592 | tf_op jit(solution)/shard_map/all_gather | solution.py:93
  42.4 44.9 %all-gather.22.cloned.1.call-done = bf16[1,2,128,4096]{3,2,1,0:T(8,128)(2,1)} async-done(((bf16[1,2,32,4096]{3,2,1,0:T(8,128)(2,1)}), bf16[1,2,128,4096]{3,2,1,0:T(8,128)(2,1)}) %all-gather.22.cloned.1.call-update) | async-done | bytes 2097168 | tf_op jit(solution)/shard_map/all_gather | solution.py:87
  88.8 51.8 %all-gather.14.cloned.1.call-done = bf16[1,2,4096,256]{3,2,1,0:T(8,128)(2,1)} async-done(((bf16[1,2,1024,256]{3,2,1,0:T(8,128)(2,1)}), bf16[1,2,4096,256]{3,2,1,0:T(8,128)(2,1)}) %all-gather.14.cloned.1.call-update) | async-done | bytes 4194320 | tf_op jit(solution)/shard_map/all_gather | solution.py:83
  140.6 6.3 dynamic-slice_bitcast_fusion.7
  155.3 39.7 %all-gather.12.cloned.1.call-done = bf16[1,2,4096,256]{3,2,1,0:T(8,128)(2,1)} async-done(((bf16[1,2,1024,256]{3,2,1,0:T(8,128)(2,1)}), bf16[1,2,4096,256]{3,2,1,0:T(8,128)(2,1)}) %all-gather.12.cloned.1.call-update) | async-done | bytes 4194320 | tf_op jit(solution)/shard_map/all_gather | solution.py:84
  205.8 148.4 %all-gather.16.cloned.1.call-done = bf16[1,2,4096,1024]{3,2,1,0:T(8,128)(2,1)} async-done(((bf16[1,2,1024,1024]{3,2,1,0:T(8,128)(2,1)}), bf16[1,2,4096,1024]{3,2,1,0:T(8,128)(2,1)}) %all-gather.16.cloned.1.call-update) | async-done | bytes 16777232 | tf_op jit(solution)/shard_map/all_gather | solution.py:82
  354.2 23.2 %dynamic-slice_bitcast_fusion.2 = (bf16[1024,4096]{0,1:T(8,128)(2,1)}, bf16[1024,4096]{0,1:T(8,128)(2,1)}, bf16[1024,4096]{0,1:T(8,128)(2,1)}, bf16[1024,4096]{0,1:T(8,128)(2,1)}) fusion(bf16[1,2,4096,1024]{3,2,1,0:T(8,128)(2,1)} %all-gather.16.cloned.1.call-done, s32[]{:T(128)S(6)} %select_n.150, s32[]{:T(128)S(6)} %select_n.145, s32[]{:T(128)S(6)} %select_n.140, ...), kind=kLoop, calls=%fused_computation.18 | loop fusion | bytes 67108880 | tf_op jit(solution)/shard_map/jvp()/dot_general | solution.py:47
  377.3 12.5 %copy.63 = bf16[1024,4096]{1,0:T(8,128)(2,1)} copy(bf16[1024,4096]{0,1:T(8,128)(2,1)} %get-tuple-element.9) | data formatting | bytes 16777216 | tf_op jit(solution)/shard_map/jvp()/dot_general | solution.py:47
  389.8 8.0 fusion.123
  400.9 141.4 %all-gather.18.cloned.1.call-done = bf16[1,2,1024,4096]{3,2,1,0:T(8,128)(2,1)} async-done(((bf16[1,2,1024,1024]{3,2,1,0:T(8,128)(2,1)}), bf16[1,2,1024,4096]{3,2,1,0:T(8,128)(2,1)}) %all-gather.18.cloned.1.call-update) | async-done | bytes 16777232 | tf_op jit(solution)/shard_map/all_gather | solution.py:85
  542.4 6.0 fusion.90
  550.3 6.4 fusion.24
  571.4 11.9 %copy.45 = bf16[1024,4096]{1,0:T(8,128)(2,1)} copy(bf16[1024,4096]{0,1:T(8,128)(2,1)} %get-tuple-element.11) | data formatting | bytes 16777216 | tf_op jit(solution)/shard_map/dot_general | solution.py:47
  583.3 11.7 %copy.72 = bf16[1024,4096]{1,0:T(8,128)(2,1)} copy(bf16[1024,4096]{0,1:T(8,128)(2,1)} %get-tuple-element.8) | data formatting | bytes 16777216 | tf_op jit(solution)/shard_map/jvp()/dot_general | solution.py:47
  622.5 13.6 %reduce-scatter.5.cloned.1.call-done = bf16[32,4096]{1,0:T(8,128)(2,1)} async-done(((bf16[128,4096]{1,0:T(8,128)(2,1)}), bf16[32,4096]{1,0:T(8,128)(2,1)}) %reduce-scatter.5.cloned.1.call-update) | async-done | bytes 262160 | tf_op jit(solution)/shard_map/reduce_scatter | solution.py:128
  639.6 12.0 %copy.54 = bf16[1024,4096]{1,0:T(8,128)(2,1)} copy(bf16[1024,4096]{0,1:T(8,128)(2,1)} %get-tuple-element.10) | data formatting | bytes 16777216 | tf_op jit(solution)/shard_map/dot_general | solution.py:47
  653.3 11.4 %all-gather.24.cloned.1.call-done = bf16[128,4096]{1,0:T(8,128)(2,1)} async-done(((bf16[32,4096]{1,0:T(8,128)(2,1)}), bf16[128,4096]{1,0:T(8,128)(2,1)}) %all-gather.24.cloned.1.call-update) | async-done | bytes 1048592 | tf_op jit(solution)/shard_map/all_gather | solution.py:94
  664.8 6.6 fusion.93
  677.4 17.0 %all-gather.20.cloned.1.call-done = bf16[128,4096]{1,0:T(8,128)(2,1)} async-done(((bf16[32,4096]{1,0:T(8,128)(2,1)}), bf16[128,4096]{1,0:T(8,128)(2,1)}) %all-gather.20.cloned.1.call-update) | async-done | bytes 1048592 | tf_op jit(solution)/shard_map/all_gather | solution.py:93
  699.2 5.9 fusion.129
  716.8 6.6 fusion.27
  726.4 13.6 %reduce-scatter.7.cloned.1.call-done = bf16[32,4096]{1,0:T(8,128)(2,1)} async-done(((bf16[128,4096]{1,0:T(8,128)(2,1)}), bf16[32,4096]{1,0:T(8,128)(2,1)}) %reduce-scatter.7.cloned.1.call-update) | async-done | bytes 262160 | tf_op jit(solution)/shard_map/reduce_scatter | solution.py:128
  741.2 27.1 %reduce-scatter.11.cloned.1.call-done = bf16[32,4096]{1,0:T(8,128)(2,1)} async-done(((bf16[128,4096]{1,0:T(8,128)(2,1)}), bf16[32,4096]{1,0:T(8,128)(2,1)}) %reduce-scatter.11.cloned.1.call-update) | async-done | bytes 262160 | tf_op jit(solution)/shard_map/reduce_scatter | solution.py:131
  769.5 75.4 %psum.7 = f32[1,2,4096]{2,1,0:T(2,128)} all-reduce(f32[1,2,4096]{2,1,0:T(2,128)S(1)} %add_bitcast_fusion), channel_id=1, replica_groups=mesh['dp'=4,'section'=2,'tensor'=4] {'dp','tensor'}, use_global_device_ids=true, to_apply=%region_22.23 | all-reduce | flops 8192 | bytes 65536 | tf_op jit(solution)/shard_map/psum | solution.py:140
  (301 shorter events, 116.3 us)
Async XLA Ops:
  7.2 33.1 %all-gather.26.cloned.1.call-start = ((), (), s32[]{:S(2)}) async-start(), calls=%async_computation.15 | async-start | bytes 1310720 | tf_op jit(solution)/shard_map/all_gather | solution.py:93
  7.9 79.4 %all-gather.22.cloned.1.call-start = ((), (), s32[]{:S(2)}) async-start(), calls=%async_computation.11 | async-start | bytes 2621440 | tf_op jit(solution)/shard_map/all_gather | solution.py:87
  8.6 131.9 %all-gather.14.cloned.1.call-start = ((), (), s32[]{:S(2)}) async-start(), calls=%async_computation.5 | async-start | bytes 5242880 | tf_op jit(solution)/shard_map/all_gather | solution.py:83
  9.4 185.6 %all-gather.12.cloned.1.call-start = ((), (), s32[]{:S(2)}) async-start(), calls=%async_computation.4 | async-start | bytes 5242880 | tf_op jit(solution)/shard_map/all_gather | solution.py:84
  10.0 344.2 %all-gather.16.cloned.1.call-start = ((), (), s32[]{:S(2)}) async-start(), calls=%async_computation.6 | async-start | bytes 20971520 | tf_op jit(solution)/shard_map/all_gather | solution.py:82
  10.5 390.4 %all-gather.28.cloned.1.call-start = ((), (), s32[]{:S(2)}) async-start(), calls=%async_computation.16 | async-start | bytes 1310720 | tf_op jit(solution)/shard_map/all_gather | solution.py:94
  11.1 531.2 %all-gather.18.cloned.1.call-start = ((), (), s32[]{:S(2)}) async-start(), calls=%async_computation.7 | async-start | bytes 20971520 | tf_op jit(solution)/shard_map/all_gather | solution.py:85
  11.9 605.2 %reduce-scatter.9.cloned.1.call-start = ((), (), s32[]{:S(2)}) async-start(), calls=%async_computation.12 | async-start | bytes 1310720 | tf_op jit(solution)/shard_map/reduce_scatter | solution.py:131
  20.4 174.6 %copy-start.39 = (f32[1,1,4096]{2,1,0:T(1,128)}, f32[1,1,4096]{2,1,0:T(1,128)S(1)}, u32[]{:S(2)}) copy-start(f32[1,1,4096]{2,1,0:T(1,128)S(1)} %get-tuple-element.40) | copy-start | bytes 49156
  88.8 58.1 %copy-start.60 = (f32[128]{0:T(128)}, f32[128]{0:T(128)S(1)}, u32[]{:S(2)}) copy-start(f32[128]{0:T(128)S(1)} %fusion.47) | copy-start | bytes 1540
  88.8 106.2 %copy-start.58 = (f32[128]{0:T(128)}, f32[128]{0:T(128)S(1)}, u32[]{:S(2)}) copy-start(f32[128]{0:T(128)S(1)} %fusion.209) | copy-start | bytes 1540
  560.3 34.8 %copy-start.65 = (f32[128]{0:T(128)}, f32[128]{0:T(128)S(1)}, u32[]{:S(2)}) copy-start(f32[128]{0:T(128)S(1)} %get-tuple-element.7) | copy-start | bytes 1540
  561.9 74.2 %reduce-scatter.5.cloned.1.call-start = ((), (), s32[]{:S(2)}) async-start(), calls=%async_computation.8 | async-start | bytes 1310720 | tf_op jit(solution)/shard_map/reduce_scatter | solution.py:128
  608.8 56.0 %all-gather.24.cloned.1.call-start = ((), (), s32[]{:S(2)}) async-start(), calls=%async_computation.13 | async-start | bytes 1310720 | tf_op jit(solution)/shard_map/all_gather | solution.py:94
  618.2 2.9 collective-permute-start.2
  621.8 72.5 %all-gather.20.cloned.1.call-start = ((), (), s32[]{:S(2)}) async-start(), calls=%async_computation.9 | async-start | bytes 1310720 | tf_op jit(solution)/shard_map/all_gather | solution.py:93
  637.9 14.4 %collective-permute-start = (bf16[32,4096]{1,0:T(8,128)(2,1)}, bf16[32,4096]{1,0:T(8,128)(2,1)S(1)}, u32[]{:S(2)}, u32[]{:S(2)}) collective-permute-start(bf16[32,4096]{1,0:T(8,128)(2,1)} %fusion.146), channel_id=1, source_target_pairs={{0,4},{4,0},{1,5},{5,1},{2,6},{6,2},{3,7},{7,3},{8,12},{12,8},{9,1... | collective-permute-start | bytes 786440 | tf_op jit(solution)/shard_map/ppermute | solution.py:18
  653.0 20.4 %copy-start.44 = (f32[2,4,128]{2,1,0:T(4,128)S(1)}, f32[2,4,128]{2,1,0:T(4,128)}, u32[]{:S(2)}) copy-start(f32[2,4,128]{2,1,0:T(4,128)} %get-tuple-element.71) | copy-start | bytes 12292
  653.1 87.0 %reduce-scatter.7.cloned.1.call-start = ((), (), s32[]{:S(2)}) async-start(), calls=%async_computation.10 | async-start | bytes 1310720 | tf_op jit(solution)/shard_map/reduce_scatter | solution.py:128
  713.3 55.0 %reduce-scatter.11.cloned.1.call-start = ((), (), s32[]{:S(2)}) async-start(), calls=%async_computation.14 | async-start | bytes 1310720 | tf_op jit(solution)/shard_map/reduce_scatter | solution.py:131
  724.8 43.5 %copy-start.13 = (bf16[32,4096]{1,0:T(8,128)(2,1)S(1)}, bf16[32,4096]{1,0:T(8,128)(2,1)}, u32[]{:S(2)}) copy-start(bf16[32,4096]{1,0:T(8,128)(2,1)} %copy-done.12) | copy-start | bytes 786436
  726.4 43.0 %copy-start.50 = (f32[4096]{0:T(1024)S(1)}, f32[4096]{0:T(1024)}, u32[]{:S(2)}) copy-start(f32[4096]{0:T(1024)} %get-tuple-element.3) | copy-start | bytes 49156
  741.1 103.9 %collective-permute-start.1 = (bf16[32,4096]{1,0:T(8,128)(2,1)S(1)}, bf16[32,4096]{1,0:T(8,128)(2,1)S(1)}, u32[]{:S(2)}, u32[]{:S(2)}) collective-permute-start(bf16[32,4096]{1,0:T(8,128)(2,1)S(1)} %add_convert_fusion.1), channel_id=1, source_target_pairs={{0,4},{4,0},{1,5},{5,1},{2,6},{6,2},{3,7},{7,3},{8,12},{12,8},{9,1... | collective-permute-start | bytes 786440 | tf_op jit(solution)/shard_map/ppermute | solution.py:18
  769.3 75.6 %collective-permute-start.3 = (bf16[32,4096]{1,0:T(8,128)(2,1)S(1)}, bf16[32,4096]{1,0:T(8,128)(2,1)S(1)}, u32[]{:S(2)}, u32[]{:S(2)}) collective-permute-start(bf16[32,4096]{1,0:T(8,128)(2,1)S(1)} %add_convert_fusion), channel_id=1, source_target_pairs={{0,4},{4,0},{1,5},{5,1},{2,6},{6,2},{3,7},{7,3},{8,12},{12,8},{9,1... | collective-permute-start | bytes 786440 | tf_op jit(solution)/shard_map/ppermute | solution.py:18
  (60 other events, 277.0 us)
Sparse Core Ops, SparseCore 0:
  9.6 30.6 all-gather.25
  41.8 45.4 all-gather.21
  89.1 51.4 all-gather.13
  142.3 52.6 all-gather.11
  196.7 157.4 all-gather.15
  355.6 27.9 all-gather.27
  385.4 156.9 all-gather.17
  562.0 27.1 reduce-scatter.8
  608.9 27.2 reduce-scatter.4
  638.1 26.5 all-gather.23
  666.9 27.4 all-gather.19
  713.4 26.6 reduce-scatter.6
  742.5 25.8 reduce-scatter.10
where the time goes:
time: 861 us; the launch traced here: 853 us
  waiting for transfers between devices  533 us (62%)
  local copies, waits for them, and re-layouts  107 us (12%)
  matrix products  96.6 us (11%)
  blocking collectives  75.4 us (9%)
  other arithmetic  24.1 us (3%)
  between operations  15.5 us (2%)
    all_gather x1, waiting for transfers between devices, per_device(): lax.all_gather(w_query, 'dp', axis=2, tiled=True)  148 us
    all_gather x1, waiting for transfers between devices, per_device(): lax.all_gather(w_out, 'dp', axis=3, tiled=True)  141 us
    psum x1, blocking collectives, per_device(): gain_total = lax.psum(gain_sum, ('dp', 'tensor'))  75.4 us
    dot_general x5, local copies, waits for them, and re-layouts, partial_layer(): jnp.dot(normed, w_query, preferred_element_type=jnp.float32)  71.3 us
    all_gather x1, waiting for transfers between devices, per_device(): lax.all_gather(w_key, 'dp', axis=2, tiled=True)  51.8 us
    all_gather x1, waiting for transfers between devices, per_device(): stash_full = lax.all_gather(stash, 'tensor', axis=2, tiled=True)  44.9 us
    all_gather x1, waiting for transfers between devices, per_device(): lax.all_gather(w_value, 'dp', axis=2, tiled=True)  39.7 us
    dot_general x6, matrix products, partial_layer(): jnp.dot(normed, w_query, preferred_element_type=jnp.float32)  38.6 us
  transfers between devices with their start and end apart: 17, of which 11 were waited for; matrix products, arithmetic and copies ran while one was open for 21% of the time, Pallas kernels for 0%

commit v1 on v0

v1 whole, which is shorter than its diff:
```python
import functools
import math

import jax
import jax.numpy as jnp
from jax import lax
from jax.experimental import pallas as pl
from jax.experimental.pallas import tpu as pltpu
from jax.sharding import PartitionSpec as P

HD = 128
TICKS = 2
ROPE_BASE = 1000000.0
MESH = pl.DeviceIdType.MESH
F32 = jnp.float32
BF16 = jnp.bfloat16

WIDE = ("in", "out")


def exchange_kernel(kinds, n_dp, n_tensor, *refs):
    count = len(kinds)
    sources, targets = refs[:count], refs[count : 2 * count]
    send_sem, recv_sem, local_sem = refs[2 * count :]
    my_dp, my_tensor = lax.axis_index("dp"), lax.axis_index("tensor")
    wide = any(kind in WIDE for kind in kinds)
    n_all = n_dp * n_tensor
    me = my_dp * n_tensor + my_tensor

    def wide_peer(step):
        peer = lax.rem(me + step, n_all)
        return peer // n_tensor, lax.rem(peer, n_tensor)

    def narrow_peer(step):
        return lax.rem(my_dp + step, n_dp), my_tensor

    barrier = pltpu.get_barrier_semaphore()
    total = n_all if wide else n_dp
    pick = wide_peer if wide else narrow_peer

    @pl.loop(1, total)
    def greet(step):
        peer_dp, peer_tensor = pick(step)
        pl.semaphore_signal(
            barrier, inc=1, device_id={"dp": peer_dp, "tensor": peer_tensor}, device_id_type=MESH
        )

    pl.semaphore_wait(barrier, total - 1)

    def block(job, peer_dp, peer_tensor):
        kind = kinds[job]
        if kind == "ag":
            return sources[job]
        if kind == "out":
            return sources[job].at[peer_dp, peer_tensor]
        return sources[job].at[peer_dp]

    def place(job):
        if kinds[job] in WIDE:
            return targets[job].at[my_dp, my_tensor]
        return targets[job].at[my_dp]

    def remote(job, step):
        peer_dp, peer_tensor = wide_peer(step) if kinds[job] in WIDE else narrow_peer(step)
        return pltpu.make_async_remote_copy(
            src_ref=block(job, peer_dp, peer_tensor),
            dst_ref=place(job),
            send_sem=send_sem.at[job, step],
            recv_sem=recv_sem.at[job, step],
            device_id={"dp": peer_dp, "tensor": peer_tensor},
            device_id_type=MESH,
        )

    def local(job):
        return pltpu.make_async_copy(block(job, my_dp, my_tensor), place(job), local_sem.at[job])

    for job in range(count):

        @pl.loop(1, n_all if kinds[job] in WIDE else n_dp)
        def send(step, job=job):
            remote(job, step).start()

    for job in range(count):
        local(job).start()
    for job in range(count):
        local(job).wait()
    for job in range(count):

        @pl.loop(1, n_all if kinds[job] in WIDE else n_dp)
        def finish(step, job=job):
            remote(job, step).wait()


def exchange(collective_id, *jobs):
    n_dp, n_tensor = lax.axis_size("dp"), lax.axis_size("tensor")
    kinds = tuple(kind for kind, _ in jobs)
    arrays = [value for _, value in jobs]
    shapes = []
    for kind, value in jobs:
        lead = {
            "in": (n_dp, n_tensor) + value.shape[1:],
            "out": value.shape,
            "rs": value.shape,
            "ag": (n_dp,) + value.shape,
        }[kind]
        shapes.append(jax.ShapeDtypeStruct(lead, value.dtype))
    count = len(jobs)
    most = n_dp * n_tensor if any(kind in WIDE for kind in kinds) else n_dp
    return pl.pallas_call(
        functools.partial(exchange_kernel, kinds, n_dp, n_tensor),
        out_shape=shapes,
        in_specs=[pl.BlockSpec(memory_space=pl.ANY)] * count,
        out_specs=[pl.BlockSpec(memory_space=pl.ANY)] * count,
        scratch_shapes=[
            pltpu.SemaphoreType.DMA((count, most)),
            pltpu.SemaphoreType.DMA((count, most)),
            pltpu.SemaphoreType.DMA((count,)),
        ],
        compiler_params=pltpu.CompilerParams(
            collective_id=collective_id, has_side_effects=True
        ),
        name="exchange_" + "_".join(kinds),
    )(*arrays)


def from_behind(value, axis, steps):
    count = lax.axis_size(axis)
    pairs = [(source, (source + steps) % count) for source in range(count)]
    return lax.ppermute(value, axis, pairs)


def rope_tables(segments):
    count_rows = segments.shape[0]
    row_index = jnp.arange(count_rows, dtype=jnp.int32)
    allowed = (segments[:, None] == segments[None, :]) & (row_index[:, None] >= row_index[None, :])
    positions = jnp.sum(allowed.astype(F32), axis=1) - 1.0
    halfway = HD // 2
    frequency = jnp.exp(jnp.arange(halfway, dtype=F32) * (-2.0 * math.log(ROPE_BASE) / HD))
    angles = positions[:, None] * frequency[None, :]
    cosine = jnp.concatenate([jnp.cos(angles), jnp.cos(angles)], axis=1)
    sine_table = jnp.concatenate([jnp.sin(angles), jnp.sin(angles)], axis=1)
    return (cosine[:, None, :], sine_table[:, None, :], allowed)


def rotate(vectors, cosine, sine_table):
    halfway = vectors.shape[-1] // 2
    turned = jnp.concatenate([-vectors[..., halfway:], vectors[..., :halfway]], axis=-1)
    return vectors * cosine + turned * sine_table


def attention(projected, widths, tables):
    cosine, sine_table, allowed = tables
    count_rows = projected.shape[0]
    query_width, key_width = widths
    query_rows = projected[:, :query_width].reshape(count_rows, -1, HD)
    key_rows = projected[:, query_width : query_width + key_width].reshape(count_rows, -1, HD)
    value_rows = projected[:, query_width + key_width :].astype(BF16).reshape(count_rows, -1, HD)
    query_rows = rotate(query_rows, cosine, sine_table).astype(BF16)
    key_rows = rotate(key_rows, cosine, sine_table).astype(BF16)
    key_heads = key_rows.shape[1]
    grouped = query_rows.reshape(count_rows, key_heads, -1, HD)
    scores = jnp.einsum("qkgd,skd->kgqs", grouped.astype(F32), key_rows.astype(F32))
    scores = scores * (1.0 / math.sqrt(HD))
    scores = jnp.where(allowed[None, None], scores, -1e30)
    exponents = jnp.exp(scores)
    soft_weights = (exponents / jnp.sum(exponents, axis=-1, keepdims=True)).astype(BF16)
    mixed_heads = jnp.einsum("kgqs,skd->qkgd", soft_weights.astype(F32), value_rows.astype(F32))
    return mixed_heads.astype(BF16).reshape(count_rows, -1)


def normalise(rows, gain_vector):
    variance = jnp.mean(rows * rows, axis=1, keepdims=True)
    return rows * lax.rsqrt(variance + 1e-06) * gain_vector


def pick_span(table, span):
    return lax.dynamic_index_in_dim(table, span, 0, keepdims=False)


def dot_t(left, right):
    return lax.dot_general(left, right, (((1,), (1,)), ((), ())), preferred_element_type=F32)


def per_device(
    fwd_state, bwd_state, stash, gains, w_query, w_key, w_value, w_out, fwd_segments, bwd_segments
):
    n_dp, n_tensor = lax.axis_size("dp"), lax.axis_size("tensor")
    phase_count = lax.axis_size("section")
    phase_index = lax.axis_index("section")
    own_rows, model_width = fwd_state.shape[1:]
    part = model_width // n_dp
    replica_rows = own_rows * n_tensor
    all_rows = replica_rows * n_dp
    widths = (w_query.shape[3], w_key.shape[3])

    def columns(rows):
        return rows.reshape(own_rows, n_dp, part).transpose(1, 0, 2)

    def project(normed, span):
        normed = normed.reshape(all_rows, part)
        pieces = [
            jnp.dot(normed, pick_span(weight[0], span), preferred_element_type=F32).astype(BF16)
            for weight in (w_query, w_key, w_value)
        ]
        return jnp.concatenate(pieces, axis=1).reshape(n_dp, replica_rows, -1)

    def summed(pieces):
        return jnp.sum(pieces.astype(F32), axis=0)

    def to_owners(term):
        return term.astype(BF16).reshape(n_dp, n_tensor, own_rows, part)

    def rows_of(pieces):
        return jnp.sum(pieces.astype(F32), axis=1).transpose(1, 0, 2).reshape(own_rows, model_width)

    gains32 = gains[0].astype(F32)
    my_part = lax.dynamic_slice_in_dim(gains32, lax.axis_index("dp") * part, part, axis=1)
    stash32 = stash[0].astype(F32)
    fwd_spans = [jnp.where(phase_index < tick, 1, 0).astype(jnp.int32) for tick in range(TICKS)]
    bwd_spans = [
        jnp.where(phase_index > phase_count - 1 - tick, 0, 1).astype(jnp.int32)
        for tick in range(TICKS)
    ]
    fwd_tables = [
        rope_tables(pick_span(fwd_segments[:, 0], (phase_index - tick) % phase_count))
        for tick in range(TICKS)
    ]
    bwd_tables = [
        rope_tables(pick_span(bwd_segments[:, 0], (phase_index + tick) % phase_count))
        for tick in range(TICKS)
    ]

    def forward_in(state_rows, tick):
        gain = pick_span(gains32, fwd_spans[tick])
        return columns(normalise(state_rows.astype(F32), gain).astype(BF16))

    def stash_in(tick):
        gain = pick_span(gains32, bwd_spans[tick])
        return columns(normalise(stash32[tick], gain).astype(BF16))

    def forward_out(mixed, tick):
        mixed = mixed.reshape(all_rows, -1)
        return to_owners(
            jnp.dot(mixed, pick_span(w_out[0], fwd_spans[tick]), preferred_element_type=F32)
        )

    def mixed_gradient(grad, tick):
        grad = grad.reshape(all_rows, part)
        return (
            dot_t(grad, pick_span(w_out[0], bwd_spans[tick]))
            .astype(BF16)
            .reshape(n_dp, replica_rows, -1)
        )

    def attention_gradient(projected, mixed_grad, tick):
        _, pull = jax.vjp(lambda x: attention(x, widths, bwd_tables[tick]), projected)
        return pull(mixed_grad.astype(BF16))[0].astype(BF16)

    def normed_gradient(gradient, normed, tick):
        gradient = gradient.reshape(all_rows, -1)
        span = bwd_spans[tick]
        query_width, key_width = widths
        term = (
            dot_t(gradient[:, :query_width], pick_span(w_query[0], span))
            + dot_t(gradient[:, query_width : query_width + key_width], pick_span(w_key[0], span))
            + dot_t(gradient[:, query_width + key_width :], pick_span(w_value[0], span))
        )
        gain_term = jnp.sum(term * normed.reshape(all_rows, part).astype(F32), axis=0)
        gain_term = gain_term / pick_span(my_part, span)
        gain_term = jnp.broadcast_to(gain_term.reshape(1, -1, 128), (n_dp, part // 128, 128))
        return to_owners(term), gain_term

    def returned_rows(grad_rows, pieces, tick):
        gain = pick_span(gains32, bwd_spans[tick])
        _, pull = jax.vjp(lambda rows: normalise(rows, gain), stash32[tick])
        return (grad_rows.astype(F32) + pull(rows_of(pieces))[0]).astype(BF16)

    span_ids = jnp.arange(2, dtype=jnp.int32)

    def gain_rows(pieces, tick):
        gain = jnp.sum(pieces, axis=1).reshape(model_width)
        chosen = (span_ids == bwd_spans[tick]).astype(F32)
        return chosen[:, None] * gain[None, :]

    state_rows, grad_rows = fwd_state[0], bwd_state[0]
    state, stash0, grad = exchange(
        0, ("in", forward_in(state_rows, 0)), ("in", stash_in(0)), ("in", columns(grad_rows))
    )
    fwd_proj, bwd_proj, mixed_grad, stash1 = exchange(
        1,
        ("rs", project(state, fwd_spans[0])),
        ("rs", project(stash0, bwd_spans[0])),
        ("rs", mixed_gradient(grad, 0)),
        ("in", stash_in(1)),
    )
    mixed = attention(summed(fwd_proj), widths, fwd_tables[0])
    gradient = attention_gradient(summed(bwd_proj), summed(mixed_grad), 0)
    mixed, gradient, bwd_proj = exchange(
        2, ("ag", mixed), ("ag", gradient), ("rs", project(stash1, bwd_spans[1]))
    )
    term, gain_term = normed_gradient(gradient, stash0, 0)
    fwd_pieces, bwd_pieces, gain0 = exchange(
        3, ("out", forward_out(mixed, 0)), ("out", term), ("in", gain_term)
    )
    advanced = (state_rows.astype(F32) + rows_of(fwd_pieces)).astype(BF16)
    state_rows = from_behind(advanced, "section", 1)
    grad_rows = from_behind(returned_rows(grad_rows, bwd_pieces, 0), "section", -1)

    state, grad = exchange(4, ("in", forward_in(state_rows, 1)), ("in", columns(grad_rows)))
    fwd_proj, mixed_grad = exchange(
        5, ("rs", project(state, fwd_spans[1])), ("rs", mixed_gradient(grad, 1))
    )
    mixed = attention(summed(fwd_proj), widths, fwd_tables[1])
    gradient = attention_gradient(summed(bwd_proj), summed(mixed_grad), 1)
    mixed, gradient = exchange(6, ("ag", mixed), ("ag", gradient))
    term, gain_term = normed_gradient(gradient, stash1, 1)
    fwd_pieces, bwd_pieces, gain1 = exchange(
        7, ("out", forward_out(mixed, 1)), ("out", term), ("in", gain_term)
    )
    advanced = (state_rows.astype(F32) + rows_of(fwd_pieces)).astype(BF16)
    state_rows = from_behind(advanced, "section", 1)
    grad_rows = from_behind(returned_rows(grad_rows, bwd_pieces, 1), "section", -1)
    gain_total = gain_rows(gain0, 0) + gain_rows(gain1, 1)
    return (state_rows[None], grad_rows[None], gain_total[None])


def solution(mesh):
    in_specs = (
        P("section", ("dp", "tensor"), None),
        P("section", ("dp", "tensor"), None),
        P("section", None, ("dp", "tensor"), None),
        P("section", None, None),
        P("section", None, "dp", "tensor"),
        P("section", None, "dp", "tensor"),
        P("section", None, "dp", "tensor"),
        P("section", None, "tensor", "dp"),
        P(None, "dp", None),
        P(None, "dp", None),
    )
    out_specs = (
        P("section", ("dp", "tensor"), None),
        P("section", ("dp", "tensor"), None),
        P("section", None, None),
    )
    return jax.shard_map(
        per_device, mesh=mesh, in_specs=in_specs, out_specs=out_specs, check_vma=False
    )
```

time: 861 us -> 568 us (0.66)
  waiting for transfers between devices: 533 us -> 0.46 us
  Pallas kernels: 0 us -> 406 us
  blocking collectives: 75.4 us -> 0 us
  local copies, waits for them, and re-layouts: 107 us -> 42.6 us
  matrix products: 96.6 us -> 67.7 us
  other arithmetic: 24.1 us -> 47.3 us
  between operations: 15.5 us -> 2.13 us
    all_gather x9 -> x0, waiting for transfers between devices: 474 us -> none  [the longest x1 148 us: per_device(): lax.all_gather(w_query, 'dp', axis=2, tiled=True)]
    pallas_call x0 -> x8, Pallas kernels: none -> 406 us  [exchange(): pl.pallas_call(functools.partial(exchange_kernel, kinds, n_dp, n_tensor),...]
    dot_general x10 -> x0, local copies, waits for them, and re-layouts: 93.2 us -> none  [the longest x5 71.3 us: partial_layer(): jnp.dot(normed, w_query, preferred_element_type=jnp.float32)]
    psum x1 -> x0, blocking collectives: 75.4 us -> none  [per_device(): gain_total = lax.psum(gain_sum, ('dp', 'tensor'))]
    reduce_scatter x4 -> x0, waiting for transfers between devices: 54.4 us -> none  [the longest x2 27.2 us: per_device(): lax.psum_scatter(forward_term.astype(jnp.bfloat16), 'tensor', scatter_dim...]
    dot_general x36, matrix products: 96.6 us -> 67.7 us  [the longest x8 24.1 us: dot_t(): lax.dot_general(left, right, (((1,), (1,)), ((), ())), preferred_element_...]
    reduce_sum x3 -> x21, other arithmetic: 4.55 us -> 17.1 us  [the longest x6 7.55 us: summed(): return jnp.sum(pieces.astype(F32), axis=0)]
  transfers between devices with their start and end apart: 17 -> 4, of which waited for: 11 -> 1; matrix products, arithmetic and copies ran while one was open for 21% -> 5% of each run, Pallas kernels for 0% -> 0%
where the time goes in v1:
time: 568 us; the launch traced here: 566 us
  Pallas kernels  406 us (71%)
  matrix products  67.7 us (12%)
  other arithmetic  47.3 us (8%)
  local copies, waits for them, and re-layouts  42.6 us (8%)
    pallas_call x8, Pallas kernels, exchange(): pl.pallas_call(functools.partial(exchange_kernel, kinds, n_dp, n_tensor),...  406 us
    dot_general x8, matrix products, dot_t(): lax.dot_general(left, right, (((1,), (1,)), ((), ())), preferred_element_...  24.1 us
    dot_general x12, matrix products, project(): jnp.dot(normed, pick_span(weight[0], span), preferred_element_type=F32)  22.4 us
  transfers between devices with their start and end apart: 4, of which 1 were waited for; matrix products, arithmetic and copies ran while one was open for 5% of the time, Pallas kernels for 0%

profile of v1, /device:TPU:0, one launch (start us, length us, event | category | flops | bytes accessed | tf_op | source)
XLA Modules:
  0.0 566.4 jit_solution(6614759900824239033)
XLA Ops:
  14.4 75.2 %exchange_in_in_in.1 = (bf16[4,4,32,1024]{3,2,1,0:T(8,128)(2,1)}, bf16[4,4,32,1024]{3,2,1,0:T(8,128)(2,1)}, bf16[4,4,32,1024]{3,2,1,0:T(8,128)(2,1)}) custom-call(bf16[4,32,1024]{2,1,0:T(8,128)(2,1)} %fusion.138.refs_0_, bf16[4,32,1024]{2,1,0:T(8,128)(2,1)} %fusion.139.refs_1_, bf16[4,32,1024]{2,1,0:T(8,128)(2,1)} %bitcast.467), custom_call_target="tpu_custom_call" | custom-call | tf_op jit(solution)/shard_map/exchange_in_in_in/pallas_call | solution.py:109
  89.7 2.5 convolution_convert_fusion.12
  92.2 2.7 convolution_convert_fusion.13
  96.5 2.2 fusion.30
  98.7 2.3 fusion.33
  101.4 4.3 fusion.36
  109.3 64.4 %exchange_rs_rs_rs_in.1 = (bf16[4,128,1536]{2,1,0:T(8,128)(2,1)}, bf16[4,128,1536]{2,1,0:T(8,128)(2,1)}, bf16[4,128,1024]{2,1,0:T(8,128)(2,1)}, bf16[4,4,32,1024]{3,2,1,0:T(8,128)(2,1)}) custom-call(bf16[4,128,1536]{2,1,0:T(8,128)(2,1)} %bitcast.424, bf16[4,128,1536]{2,1,0:T(8,128)(2,1)} %bitcast.425, bf16[4,128,1024]{2,1,0:T(8,128)(2,1)} %bitcast.466, ...), custom_call_target="tpu_custom_call" | custom-call | tf_op jit(solution)/shard_map/exchange_rs_rs_rs_in/pallas_call | solution.py:109
  189.7 2.3 fusion.39
  202.1 48.5 %exchange_ag_ag_rs.1 = (bf16[4,128,1024]{2,1,0:T(8,128)(2,1)}, bf16[4,128,1536]{2,1,0:T(8,128)(2,1)}, bf16[4,128,1536]{2,1,0:T(8,128)(2,1)}) custom-call(bf16[128,1024]{1,0:T(8,128)(2,1)} %copy.357.refs_0_, bf16[128,1536]{1,0:T(8,128)(2,1)} %add_convert_fusion.1.refs_1_, bf16[4,128,1536]{2,1,0:T(8,128)(2,1)} %bitcast.426), custom_call_target="tpu_custom_call" | custom-call | tf_op jit(solution)/shard_map/exchange_ag_ag_rs/pallas_call | solution.py:109
  250.6 2.9 fusion.109
  253.5 4.2 fusion.14
  257.7 4.2 fusion.42
  262.0 4.0 multiply_reduce_fusion.1
  268.0 52.0 %exchange_out_out_in.2 = (bf16[4,4,32,1024]{3,2,1,0:T(8,128)(2,1)}, bf16[4,4,32,1024]{3,2,1,0:T(8,128)(2,1)}, f32[4,4,8,128]{3,2,1,0:T(8,128)}) custom-call(bf16[4,4,32,1024]{3,2,1,0:T(8,128)(2,1)} %bitcast.469, bf16[4,4,32,1024]{3,2,1,0:T(8,128)(2,1)} %bitcast.440, f32[4,8,128]{2,1,0:T(8,128)} %broadcast_in_dim.68.refs_2_), custom_call_target="tpu_custom_call" | custom-call | tf_op jit(solution)/shard_map/exchange_out_out_in/pallas_call | solution.py:109
  349.0 49.8 %exchange_in_in.1 = (bf16[4,4,32,1024]{3,2,1,0:T(8,128)(2,1)}, bf16[4,4,32,1024]{3,2,1,0:T(8,128)(2,1)}) custom-call(bf16[4,32,1024]{2,1,0:T(8,128)(2,1)} %bitcast.472, bf16[4,32,1024]{2,1,0:T(8,128)(2,1)} %bitcast.473), custom_call_target="tpu_custom_call" | custom-call | tf_op jit(solution)/shard_map/exchange_in_in/pallas_call | solution.py:109
  402.4 3.0 fusion.45
  405.5 2.4 fusion.48
  409.1 31.0 %exchange_rs_rs.1 = (bf16[4,128,1536]{2,1,0:T(8,128)(2,1)}, bf16[4,128,1024]{2,1,0:T(8,128)(2,1)}) custom-call(bf16[4,128,1536]{2,1,0:T(8,128)(2,1)} %bitcast.427, bf16[4,128,1024]{2,1,0:T(8,128)(2,1)} %bitcast.471), custom_call_target="tpu_custom_call" | custom-call | tf_op jit(solution)/shard_map/exchange_rs_rs/pallas_call | solution.py:109
  442.5 2.2 reduce_sum.324
  446.6 1.9 fusion.67
  463.8 31.0 %exchange_ag_ag.1 = (bf16[4,128,1024]{2,1,0:T(8,128)(2,1)}, bf16[4,128,1536]{2,1,0:T(8,128)(2,1)}) custom-call(bf16[128,1024]{1,0:T(8,128)(2,1)} %copy.368.refs_0_, bf16[128,1536]{1,0:T(8,128)(2,1)} %add_convert_fusion.refs_1_), custom_call_target="tpu_custom_call" | custom-call | tf_op jit(solution)/shard_map/exchange_ag_ag/pallas_call | solution.py:109
  496.6 3.0 fusion.8
  499.7 2.2 fusion.51
  504.3 53.5 %exchange_out_out_in.3 = (bf16[4,4,32,1024]{3,2,1,0:T(8,128)(2,1)}, bf16[4,4,32,1024]{3,2,1,0:T(8,128)(2,1)}, f32[4,4,8,128]{3,2,1,0:T(8,128)}) custom-call(bf16[4,4,32,1024]{3,2,1,0:T(8,128)(2,1)} %bitcast.470, bf16[4,4,32,1024]{3,2,1,0:T(8,128)(2,1)} %bitcast.441, f32[4,8,128]{2,1,0:T(8,128)} %broadcast_in_dim.74.refs_2_), custom_call_target="tpu_custom_call" | custom-call | tf_op jit(solution)/shard_map/exchange_out_out_in/pallas_call | solution.py:109
  (371 shorter events, 112.5 us)
Async XLA Ops:
  0.6 89.0 %copy-start = (bf16[1,2,1024,256]{3,2,1,0:T(8,128)(2,1)S(1)}, bf16[1,2,1024,256]{3,2,1,0:T(8,128)(2,1)}, u32[]{:S(2)}) copy-start(bf16[1,2,1024,256]{3,2,1,0:T(8,128)(2,1)} %param.16) | copy-start | bytes 3145732
  0.6 6.2 %copy-start.1 = (bf16[1,2,32,4096]{3,2,1,0:T(8,128)(2,1)S(1)}, bf16[1,2,32,4096]{3,2,1,0:T(8,128)(2,1)}, u32[]{:S(2)}) copy-start(bf16[1,2,32,4096]{3,2,1,0:T(8,128)(2,1)} %param.12) | copy-start | bytes 1572868
  2.0 176.8 %copy-start.69 = (s32[128]{0:T(128)}, s32[128]{0:T(128)S(1)}, u32[]{:S(2)}) copy-start(s32[128]{0:T(128)S(1)} %get-tuple-element.95) | copy-start | bytes 1540
  2.0 177.0 %copy-start.67 = (s32[128]{0:T(128)}, s32[128]{0:T(128)S(1)}, u32[]{:S(2)}) copy-start(s32[128]{0:T(128)S(1)} %get-tuple-element.124) | copy-start | bytes 1540
  5.7 4.1 copy-start.17
  11.0 81.2 %copy-start.75 = (f32[32]{0:T(128)}, f32[32]{0:T(128)S(1)}, u32[]{:S(2)}) copy-start(f32[32]{0:T(128)S(1)} %get-tuple-element.47) | copy-start | bytes 388
  11.0 81.2 %copy-start.77 = (f32[32]{0:T(128)}, f32[32]{0:T(128)S(1)}, u32[]{:S(2)}) copy-start(f32[32]{0:T(128)S(1)} %get-tuple-element.48) | copy-start | bytes 388
  12.4 79.8 %copy-start.73 = (f32[32]{0:T(128)}, f32[32]{0:T(128)S(1)}, u32[]{:S(2)}) copy-start(f32[32]{0:T(128)S(1)} %get-tuple-element.121) | copy-start | bytes 388
  12.4 93.3 %copy-start.71 = (f32[32]{0:T(128)}, f32[32]{0:T(128)S(1)}, u32[]{:S(2)}) copy-start(f32[32]{0:T(128)S(1)} %get-tuple-element.122) | copy-start | bytes 388
  89.6 5.2 copy-start.11
  89.6 6.9 %copy-start.86 = (bf16[4,4,32,1024]{3,2,1,0:T(8,128)(2,1)S(1)}, bf16[4,4,32,1024]{3,2,1,0:T(8,128)(2,1)}, u32[]{:S(2)}) copy-start(bf16[4,4,32,1024]{3,2,1,0:T(8,128)(2,1)} %get-tuple-element.25) | copy-start | bytes 3145732
  92.2 4.3 copy-start.82
  101.4 5.4 copy-start.15
  101.4 5.4 copy-start.34
  101.4 5.3 copy-start.35
  200.8 49.8 %copy-start.25 = (bf16[1,2,1024,256]{3,2,1,0:T(8,128)(2,1)S(1)}, bf16[1,2,1024,256]{3,2,1,0:T(8,128)(2,1)}, u32[]{:S(2)}) copy-start(bf16[1,2,1024,256]{3,2,1,0:T(8,128)(2,1)} %param.15) | copy-start | bytes 3145732
  257.7 4.2 copy-start.12
  268.0 53.7 %copy-start.4 = (bf16[1,32,4096]{2,1,0:T(8,128)(2,1)S(1)}, bf16[1,32,4096]{2,1,0:T(8,128)(2,1)}, u32[]{:S(2)}) copy-start(bf16[1,32,4096]{2,1,0:T(8,128)(2,1)} %param.10) | copy-start | bytes 786436
  322.4 21.9 %collective-permute-start = (bf16[32,4096]{1,0:T(8,128)(2,1)}, bf16[32,4096]{1,0:T(8,128)(2,1)}, u32[]{:S(2)}, u32[]{:S(2)}) collective-permute-start(bf16[32,4096]{1,0:T(8,128)(2,1)} %fusion.117), channel_id=1, source_target_pairs={{0,4},{4,0},{1,5},{5,1},{2,6},{6,2},{3,7},{7,3},{8,12},{12,8},{9,1... | collective-permute-start | bytes 786440 | tf_op jit(solution)/shard_map/ppermute | solution.py:129
  324.3 4.6 copy-start.52
  324.3 23.0 %collective-permute-start.1 = (bf16[32,4096]{1,0:T(8,128)(2,1)}, bf16[32,4096]{1,0:T(8,128)(2,1)}, u32[]{:S(2)}, u32[]{:S(2)}) collective-permute-start(bf16[32,4096]{1,0:T(8,128)(2,1)} %fusion.77), channel_id=1, source_target_pairs={{0,4},{4,0},{1,5},{5,1},{2,6},{6,2},{3,7},{7,3},{8,12},{12,8},{9,1... | collective-permute-start | bytes 786440 | tf_op jit(solution)/shard_map/ppermute | solution.py:129
  441.8 6.6 %copy-start.3 = (f32[128,1536]{1,0:T(8,128)}, f32[128,1536]{1,0:T(8,128)S(1)}, u32[]{:S(2)}) copy-start(f32[128,1536]{1,0:T(8,128)S(1)} %convert_reduce_fusion.1) | copy-start | bytes 2359300
  560.3 4.2 collective-permute-start.2
  563.3 1.7 collective-permute-start.3
  (74 other events, 156.6 us)
